TPU v7x, 256 devices: a whole 4x4x8 slice. The times are simulated.
256 devices in a mesh: segment: 4 (over y_lo, core), tp: 64 (over x, y_hi, z).
Axes of the slice: x: 4, y: 4 (y_hi: 2, y_lo: 2; y = y_hi * 2 + y_lo), z: 8, core: 2. Of those that a mesh axis runs over, the one named last changes fastest.
Arguments:
- top_grad: bfloat16 [2, 128, 4096], P(None, None, 'tp'), may hold values from -6 to 6
- saved_in: bfloat16 [2, 4, 128, 4096], P(None, 'segment', None, 'tp'), may hold values from -6 to 6
- saved_pre: bfloat16 [2, 4, 128, 16384], P(None, 'segment', None, 'tp'), may hold values from -6 to 6
- w_up: bfloat16 [2, 4, 4096, 16384], P(None, 'segment', None, 'tp'), as said below
- w_down: bfloat16 [2, 4, 16384, 4096], P(None, 'segment', 'tp'), as said below
- mask_up: int32 [2, 4, 32, 128], P(None, 'segment', None, 'tp'), may hold values from 0 to 1, as said below
- mask_down: int32 [2, 4, 128, 32], P(None, 'segment', 'tp'), may hold values from 0 to 1, as said below
Outputs:
- all_grads: bfloat16 [2, 4, 128, 4096], P(None, 'segment', None, 'tp')
- grad_up: bfloat16 [2, 4, 2048, 16384], P(None, 'segment', None, 'tp')
- grad_down: bfloat16 [2, 4, 16384, 2048], P(None, 'segment', 'tp')
Inputs may be any that keep to these rules, and one draw needn't show every extreme that they name: `mask_up`: 0 or 1; in every row, of each aligned pair of blocks along the hidden units (blocks 2j and 2j + 1) exactly one is 1; entry [1, s] equals entry [0, 3 - s]. `mask_down`: 0 or 1; in every column, of each aligned pair of blocks along the hidden units (blocks 2j and 2j + 1) exactly one is 1; entry [1, s] equals entry [0, 3 - s]. `w_up`: entry [1, s] equals entry [0, 3 - s]. `w_down`: entry [1, s] equals entry [0, 3 - s].
All inputs are finite; a program needn't handle non-finite values.
Results may differ from a plain program's by a relative error of at most 0.017.
Values may be sent and summed in bfloat16 or wider, within the bound.
No kernel may reach another device: no remote copies, remote signals or barrier semaphores. Data moves between devices by JAX's collectives and lax.ppermute only.
A program may use at most 128 MiB of HBM per device.

v0:
```python
import jax
import jax.numpy as jnp
from jax import lax
from jax.sharding import PartitionSpec as P

BLOCK = 128


def shifted(value, axis, steps):
    count = lax.axis_size(axis)
    leading, last = (max(0, -steps), min(count, count - steps))
    return lax.ppermute(value, axis, [(source, source + steps) for source in range(leading, last)])


def swapped(shard, axis, stride):
    return lax.ppermute(shard, axis, [(i, i ^ 1 << stride) for i in range(lax.axis_size(axis))])


def expand(mask):
    return jnp.repeat(jnp.repeat(mask, BLOCK, axis=-2), BLOCK, axis=-1).astype(jnp.bfloat16)


def per_device(top_grad, saved_in, saved_pre, w_up, w_down, mask_up, mask_down):
    segments = lax.axis_size("segment")
    section = lax.axis_index("segment")
    ups_mask = expand(mask_up[:, 0])
    downs_mask = expand(mask_down[:, 0])
    ups = w_up[:, 0] * ups_mask
    downs = w_down[:, 0] * downs_mask
    down_in = top_grad[0]
    up_in = top_grad[1]
    keep_grad = [None, None]
    keep_du = [None, None]
    keep_out = [None, None]
    for step in range(segments):
        down_on = section == segments - 1 - step
        up_on = section == step
        which = jnp.where(up_on, 1, 0).astype(jnp.int32)
        incoming = jnp.where(up_on, up_in, down_in)
        full_grad = lax.all_gather(incoming, "tp", axis=1, tiled=True)
        up_sel = lax.dynamic_index_in_dim(ups, which, 0, keepdims=False)
        down_sel = lax.dynamic_index_in_dim(downs, which, 0, keepdims=False)
        pre = lax.dynamic_index_in_dim(saved_pre[:, 0], which, 0, keepdims=False).astype(
            jnp.float32
        )
        dh = lax.dot_general(
            full_grad, down_sel, (((1,), (1,)), ((), ())), preferred_element_type=jnp.float32
        )
        sig = jax.nn.sigmoid(pre)
        du = (dh * sig * (1.0 + pre * (1.0 - sig))).astype(jnp.bfloat16)
        summed = lax.psum_scatter(
            lax.dot_general(
                up_sel, du, (((1,), (1,)), ((), ())), preferred_element_type=jnp.float32
            ),
            "tp",
            scatter_dimension=0,
            tiled=True,
        )
        out = (incoming.astype(jnp.float32) + summed.T).astype(jnp.bfloat16)
        for r, active in ((0, down_on), (1, up_on)):
            if keep_grad[r] is None:
                keep_grad[r] = full_grad
                keep_du[r] = du
                keep_out[r] = out
            else:
                keep_grad[r] = jnp.where(active, full_grad, keep_grad[r])
                keep_du[r] = jnp.where(active, du, keep_du[r])
                keep_out[r] = jnp.where(active, out, keep_out[r])
        if step + 1 < segments:
            down_in = shifted(out, "segment", -1)
            up_in = shifted(out, "segment", 1)
    inputs_full = lax.all_gather(saved_in[:, 0], "tp", axis=2, tiled=True)
    hidden = jax.nn.silu(saved_pre[:, 0].astype(jnp.float32)).astype(jnp.bfloat16)
    half = inputs_full.shape[2] // 2
    grads_u = []
    grads_d = []
    for r in range(2):
        g_up = jnp.dot(inputs_full[r].T, keep_du[r], preferred_element_type=jnp.float32)
        g_down = jnp.dot(hidden[r].T, keep_grad[r], preferred_element_type=jnp.float32)
        grads_u.append((g_up * ups_mask[r].astype(jnp.float32)).astype(jnp.bfloat16))
        grads_d.append((g_down * downs_mask[r].astype(jnp.float32)).astype(jnp.bfloat16))
    local_f = grads_u[0].shape[1]
    outgoing = jnp.stack(
        [
            grads_u[0][half:],
            grads_u[1][:half],
            grads_d[0][:, half:].reshape(half, local_f),
            grads_d[1][:, :half].reshape(half, local_f),
        ]
    )
    levels = segments.bit_length() - 1
    received = outgoing
    for bit in range(levels):
        received = swapped(received, "segment", bit)
    recv = received.astype(jnp.float32)
    up_low = (grads_u[0][:half].astype(jnp.float32) + recv[1]).astype(jnp.bfloat16)
    up_high = (grads_u[1][half:].astype(jnp.float32) + recv[0]).astype(jnp.bfloat16)
    down_low = (grads_d[0][:, :half].astype(jnp.float32) + recv[3].reshape(local_f, half)).astype(
        jnp.bfloat16
    )
    down_high = (grads_d[1][:, half:].astype(jnp.float32) + recv[2].reshape(local_f, half)).astype(
        jnp.bfloat16
    )
    all_grads = jnp.stack(keep_out)[:, None]
    grad_up = jnp.stack([up_low, up_high])[:, None]
    grad_down = jnp.stack([down_low, down_high])[:, None]
    return (all_grads, grad_up, grad_down)


def solution(mesh):
    return jax.shard_map(
        per_device,
        mesh=mesh,
        in_specs=(
            P(None, None, "tp"),
            P(None, "segment", None, "tp"),
            P(None, "segment", None, "tp"),
            P(None, "segment", None, "tp"),
            P(None, "segment", "tp", None),
            P(None, "segment", None, "tp"),
            P(None, "segment", "tp", None),
        ),
        out_specs=(
            P(None, "segment", None, "tp"),
            P(None, "segment", None, "tp"),
            P(None, "segment", "tp", None),
        ),
        check_vma=False,
    )
```

profile of v0, /device:TPU:8, one launch (start us, length us, event | category | flops | bytes accessed | tf_op | source)
XLA Modules:
  0.0 2104.4 jit_solution(4135660857054861701)
XLA Ops:
  7.2 1.3 slice_select_fusion
  10.4 26.2 %broadcast_in_dim.38 = bf16[2,4096,2,128]{3,2,1,0:T(2,128)(2,1)} broadcast(bf16[2,4096,2]{2,1,0:T(8,128)(2,1)S(1)} %bitcast.236), dimensions={0,1,2} | broadcast | bytes 4227072 | tf_op jit(solution)/shard_map/broadcast_in_dim | solution.py:20
  36.6 7.6 convert_element_type.200
  44.3 3.9 broadcast_in_dim.40
  48.2 7.3 convert_element_type.204
  55.5 6.2 bitcast_multiply_fusion.1
  61.7 1.3 copy-done.8
  63.0 2.4 bitcast_multiply_fusion
  65.4 62.4 %all-gather.14.cloned.1.call-done = bf16[1,128,4096]{1,2,0:T(8,128)(2,1)} async-done(((bf16[1,128,64]{1,2,0:T(8,128)(2,1)}), bf16[1,128,4096]{1,2,0:T(8,128)(2,1)}) %all-gather.14.cloned.1.call-update) | async-done | bytes 1048592 | tf_op jit(solution)/shard_map/all_gather | solution.py:40
  127.8 2.8 fusion.67
  130.6 3.6 fusion.24
  134.3 363.3 %reduce-scatter.5.cloned.1.call-done = f32[64,128]{1,0:T(8,128)} async-done(((f32[4096,128]{1,0:T(8,128)}), f32[64,128]{1,0:T(8,128)}) %reduce-scatter.5.cloned.1.call-update) | async-done | bytes 32784 | tf_op jit(solution)/shard_map/reduce_scatter | solution.py:51
  497.6 0.8 fusion.119
  498.4 1.9 collective-permute-start.1
  500.3 2.4 collective-permute-start
  502.7 2.6 collective-permute-done
  506.1 105.7 %all-gather.8.cloned.1.call-done = bf16[128,4096]{0,1:T(8,128)(2,1)} async-done(((bf16[128,64]{0,1:T(8,128)(2,1)}), bf16[128,4096]{0,1:T(8,128)(2,1)}) %all-gather.8.cloned.1.call-update) | async-done | bytes 1048592 | tf_op jit(solution)/shard_map/all_gather | solution.py:40
  611.8 2.8 fusion.64
  614.5 3.6 fusion.20
  618.2 362.6 %reduce-scatter.7.cloned.1.call-done = f32[64,128]{1,0:T(8,128)} async-done(((f32[4096,128]{1,0:T(8,128)}), f32[64,128]{1,0:T(8,128)}) %reduce-scatter.7.cloned.1.call-update) | async-done | bytes 32784 | tf_op jit(solution)/shard_map/reduce_scatter | solution.py:51
  980.8 0.8 fusion.122
  981.6 1.9 collective-permute-start.3
  983.5 2.4 collective-permute-start.2
  985.9 2.6 collective-permute-done.2
  989.3 105.7 %all-gather.10.cloned.1.call-done = bf16[128,4096]{0,1:T(8,128)(2,1)} async-done(((bf16[128,64]{0,1:T(8,128)(2,1)}), bf16[128,4096]{0,1:T(8,128)(2,1)}) %all-gather.10.cloned.1.call-update) | async-done | bytes 1048592 | tf_op jit(solution)/shard_map/all_gather | solution.py:40
  1095.0 2.8 fusion.61
  1097.7 3.6 fusion.16
  1101.4 362.6 %reduce-scatter.9.cloned.1.call-done = f32[64,128]{1,0:T(8,128)} async-done(((f32[4096,128]{1,0:T(8,128)}), f32[64,128]{1,0:T(8,128)}) %reduce-scatter.9.cloned.1.call-update) | async-done | bytes 32784 | tf_op jit(solution)/shard_map/reduce_scatter | solution.py:51
  1464.0 0.8 fusion.121
  1464.8 1.9 collective-permute-start.5
  1466.7 2.4 collective-permute-start.4
  1469.1 2.6 collective-permute-done.4
  1472.4 0.7 all-gather.16.cloned.1.call-update
  1474.2 103.9 %all-gather.12.cloned.1.call-done = bf16[128,4096]{0,1:T(8,128)(2,1)} async-done(((bf16[128,64]{0,1:T(8,128)(2,1)}), bf16[128,4096]{0,1:T(8,128)(2,1)}) %all-gather.12.cloned.1.call-update) | async-done | bytes 1048592 | tf_op jit(solution)/shard_map/all_gather | solution.py:40
  1578.2 1.1 broadcast_in_dim.49
  1580.4 2.8 fusion.3
  1583.2 1.3 copy-done.2
  1585.9 1.1 broadcast_in_dim.47
  1588.0 2.8 fusion.2
  1590.9 1.3 copy-done.3
  1593.5 2.8 fusion.58
  1596.3 100.5 %all-gather.16.cloned.1.call-done = bf16[2,1,128,4096]{2,3,1,0:T(8,128)(2,1)} async-done(((bf16[2,1,128,64]{2,3,1,0:T(8,128)(2,1)}), bf16[2,1,128,4096]{2,3,1,0:T(8,128)(2,1)}) %all-gather.16.cloned.1.call-update) | async-done | bytes 2097168 | tf_op jit(solution)/shard_map/all_gather | solution.py:72
  1697.2 1.1 copy-done.17
  1698.3 0.7 fusion.5
  1699.7 0.7 copy-done.4
  1700.4 0.7 fusion.4
  1701.3 2.3 pad_maximum_fusion
  1704.3 1.3 copy-done
  1705.6 2.0 fusion.12
  1707.6 4.1 collective-permute-done.6
  1711.8 1.4 collective-permute-start.7
  1713.2 358.0 %reduce-scatter.11.cloned.1.call-done = f32[64,128]{1,0:T(8,128)} async-done(((f32[4096,128]{1,0:T(8,128)}), f32[64,128]{1,0:T(8,128)}) %reduce-scatter.11.cloned.1.call-update) | async-done | bytes 32784 | tf_op jit(solution)/shard_map/reduce_scatter | solution.py:51
  2071.2 0.8 select_bitcast_fusion.1
  2072.6 3.4 fusion.135
  2075.9 1.9 copy.17
  2077.8 1.7 reshape_squeeze.6
  2079.5 1.5 fusion.70
  2081.0 2.9 copy.18
  2084.0 1.7 reshape_squeeze.7
  2085.7 2.5 fusion.71
  2088.2 3.4 convert_element_type.248
  2091.7 0.7 fusion.72
  2092.6 2.5 copy.20
  2095.1 2.7 maximum_bitcast_fusion.1
  (108 shorter events, 12.4 us)
Async XLA Ops:
  7.2 120.7 %all-gather.14.cloned.1.call-start = ((), (), s32[]{:S(2)}) async-start(), calls=%async_computation.11 | async-start | bytes 1064960 | tf_op jit(solution)/shard_map/all_gather | solution.py:40
  8.6 489.0 %reduce-scatter.5.cloned.1.call-start = ((), (), s32[]{:S(2)}) async-start(), calls=%async_computation.4 | async-start | bytes 2129920 | tf_op jit(solution)/shard_map/reduce_scatter | solution.py:51
  55.5 6.2 copy-start.1
  55.5 7.4 copy-start.8
  63.0 64.9 %copy-start.21 = (bf16[2,1,128,256]{3,2,1,0:T(8,128)(2,1)S(1)}, bf16[2,1,128,256]{3,2,1,0:T(8,128)(2,1)}, u32[]{:S(2)}) copy-start(bf16[2,1,128,256]{3,2,1,0:T(8,128)(2,1)} %param.9) | copy-start | bytes 393220
  134.2 363.4 %copy-start.23 = (bf16[2,128,64]{1,2,0:T(8,128)(2,1)S(1)}, bf16[2,128,64]{1,2,0:T(8,128)(2,1)}, u32[]{:S(2)}) copy-start(bf16[2,128,64]{1,2,0:T(8,128)(2,1)} %param.7) | copy-start | bytes 98308
  134.2 477.5 %all-gather.8.cloned.1.call-start = ((), (), s32[]{:S(2)}) async-start(), calls=%async_computation.5 | async-start | bytes 1064960 | tf_op jit(solution)/shard_map/all_gather | solution.py:40
  498.4 4.3 collective-permute-start.1
  500.3 5.1 collective-permute-start
  506.0 474.8 %reduce-scatter.7.cloned.1.call-start = ((), (), s32[]{:S(2)}) async-start(), calls=%async_computation.6 | async-start | bytes 2129920 | tf_op jit(solution)/shard_map/reduce_scatter | solution.py:51
  618.1 362.7 %copy-start.18 = (bf16[128,64]{0,1:T(8,128)(2,1)S(1)}, bf16[128,64]{0,1:T(8,128)(2,1)}, u32[]{:S(2)}) copy-start(bf16[128,64]{0,1:T(8,128)(2,1)} %broadcast_select_fusion) | copy-start | bytes 49156
  618.2 476.8 %all-gather.10.cloned.1.call-start = ((), (), s32[]{:S(2)}) async-start(), calls=%async_computation.7 | async-start | bytes 1064960 | tf_op jit(solution)/shard_map/all_gather | solution.py:40
  981.6 7.7 copy-start.24
  981.6 4.3 collective-permute-start.3
  983.5 5.1 collective-permute-start.2
  989.2 474.8 %reduce-scatter.9.cloned.1.call-start = ((), (), s32[]{:S(2)}) async-start(), calls=%async_computation.8 | async-start | bytes 2129920 | tf_op jit(solution)/shard_map/reduce_scatter | solution.py:51
  1101.3 362.7 %copy-start.19 = (bf16[128,64]{0,1:T(8,128)(2,1)S(1)}, bf16[128,64]{0,1:T(8,128)(2,1)}, u32[]{:S(2)}) copy-start(bf16[128,64]{0,1:T(8,128)(2,1)} %broadcast_select_fusion.1) | copy-start | bytes 49156
  1101.3 372.0 %copy-start.28 = (s32[2,1,32,2]{2,3,1,0:T(2,128)S(1)}, s32[2,1,32,2]{2,3,1,0:T(2,128)}, u32[]{:S(2)}) copy-start(s32[2,1,32,2]{2,3,1,0:T(2,128)} %param.12) | copy-start | bytes 1540
  1101.3 372.1 %copy-start.29 = (s32[2,1,2,32]{3,2,1,0:T(2,128)S(1)}, s32[2,1,2,32]{3,2,1,0:T(2,128)}, u32[]{:S(2)}) copy-start(s32[2,1,2,32]{3,2,1,0:T(2,128)} %param.13) | copy-start | bytes 1540
  1101.4 476.8 %all-gather.12.cloned.1.call-start = ((), (), s32[]{:S(2)}) async-start(), calls=%async_computation.9 | async-start | bytes 1064960 | tf_op jit(solution)/shard_map/all_gather | solution.py:40
  1464.8 8.6 copy-start.26
  1464.8 4.3 collective-permute-start.5
  1466.7 5.1 collective-permute-start.4
  1472.4 224.4 %all-gather.16.cloned.1.call-start = ((), (), s32[]{:S(2)}) async-start(), calls=%async_computation.12 | async-start | bytes 2129920 | tf_op jit(solution)/shard_map/all_gather | solution.py:72
  1473.1 598.0 %reduce-scatter.11.cloned.1.call-start = ((), (), s32[]{:S(2)}) async-start(), calls=%async_computation.10 | async-start | bytes 2129920 | tf_op jit(solution)/shard_map/reduce_scatter | solution.py:51
  1578.2 1.2 copy-start.9
  1578.2 1.5 copy-start.11
  1578.2 1.8 copy-start.13
  1578.2 2.1 copy-start.15
  1583.2 1.3 copy-start.2
  1585.1 0.7 copy-start.30
  1585.8 1.2 copy-start.10
  1585.9 1.5 copy-start.12
  1585.9 1.8 copy-start.14
  1585.9 2.1 copy-start.16
  1590.9 1.3 copy-start.3
  1592.3 1.2 copy-start.22
  1696.8 1.6 copy-start.17
  1699.1 1.3 copy-start.4
  1701.2 3.1 copy-start.6
  1701.2 4.3 copy-start
  1704.3 7.5 collective-permute-start.6
  1707.6 363.6 %copy-start.20 = (bf16[128,64]{0,1:T(8,128)(2,1)S(1)}, bf16[128,64]{0,1:T(8,128)(2,1)}, u32[]{:S(2)}) copy-start(bf16[128,64]{0,1:T(8,128)(2,1)} %broadcast_select_fusion.2) | copy-start | bytes 49156
  1707.6 363.6 %copy-start.25 = (bf16[128,64]{0,1:T(8,128)(2,1)S(1)}, bf16[128,64]{0,1:T(8,128)(2,1)}, u32[]{:S(2)}) copy-start(bf16[128,64]{0,1:T(8,128)(2,1)} %copy-done.24) | copy-start | bytes 49156
  1707.6 363.6 %copy-start.27 = (bf16[128,64]{0,1:T(8,128)(2,1)S(1)}, bf16[128,64]{0,1:T(8,128)(2,1)}, u32[]{:S(2)}) copy-start(bf16[128,64]{0,1:T(8,128)(2,1)} %copy-done.26) | copy-start | bytes 49156
  1711.8 360.8 %collective-permute-start.7 = (bf16[4,2048,256]{1,2,0:T(8,128)(2,1)}, bf16[4,2048,256]{1,2,0:T(8,128)(2,1)}, u32[]{:S(2)}, u32[]{:S(2)}) collective-permute-start(bf16[4,2048,256]{1,2,0:T(8,128)(2,1)} %collective-permute-done.6), channel_id=1, source_target_pairs={{0,128},{64,192},{128,0},{192,64},{1,129},{65,193},{129,1},{193,65... | collective-permute-start | bytes 12582920 | tf_op jit(solution)/shard_map/ppermute | solution.py:16
  2088.2 3.4 copy-start.5
  2088.2 3.5 copy-start.7
Sparse Core Ops, SparseCore 0:
  12.1 115.7 all-gather.13
  134.4 363.1 reduce-scatter.4
  506.1 105.5 all-gather.7
  618.3 362.4 reduce-scatter.6
  989.3 105.6 all-gather.9
  1101.5 362.4 reduce-scatter.8
  1472.5 105.6 all-gather.11
  1582.3 114.4 all-gather.15
  1707.7 363.3 reduce-scatter.10
where the time goes:
time: 2110 us; the launch traced here: 2100 us
  waiting for transfers between devices  1940 us (92%)
  local copies, waits for them, and re-layouts  75.5 us (4%)
  matrix products  31.1 us (1%)
  other arithmetic  30.9 us (1%)
    reduce_scatter x4, waiting for transfers between devices, per_device(): lax.psum_scatter(lax.dot_general(up_sel, du, (((1,), (1,)), ((), ())), pr...  1450 us
    all_gather x4, waiting for transfers between devices, per_device(): full_grad = lax.all_gather(incoming, 'tp', axis=1, tiled=True)  378 us
    all_gather x1, waiting for transfers between devices, per_device(): inputs_full = lax.all_gather(saved_in[:, 0], 'tp', axis=2, tiled=True)  100 us
  transfers between devices with their start and end apart: 17, of which 13 were waited for; matrix products, arithmetic and copies ran while one was open for 3% of the time, Pallas kernels for 0%

commit v1 on v0

--- a/solution.py
+++ b/solution.py
@@ -69,7 +69,9 @@
         if step + 1 < segments:
             down_in = shifted(out, "segment", -1)
             up_in = shifted(out, "segment", 1)
-    inputs_full = lax.all_gather(saved_in[:, 0], "tp", axis=2, tiled=True)
+    inputs_full = jnp.concatenate(
+        lax.all_to_all(jnp.stack([saved_in[:, 0]] * lax.axis_size("tp")), "tp", 0, 0), axis=2
+    )
     hidden = jax.nn.silu(saved_pre[:, 0].astype(jnp.float32)).astype(jnp.bfloat16)
     half = inputs_full.shape[2] // 2
     grads_u = []

time: 2110 us -> 2010 us (0.953)
  waiting for transfers between devices: 1940 us -> 1830 us
    all_gather x1 -> x0, waiting for transfers between devices: 100 us -> none  [per_device(): inputs_full = lax.all_gather(saved_in[:, 0], 'tp', axis=2, tiled=True)]
  transfers between devices with their start and end apart: 17 -> 17, of which waited for: 13 -> 12; matrix products, arithmetic and copies ran while one was open for 3% -> 3% of each run, Pallas kernels for 0% -> 0%
where the time goes in v1:
time: 2010 us
  waiting for transfers between devices  1830 us (91%)
  local copies, waits for them, and re-layouts  81 us (4%)
  matrix products  31.1 us (2%)
  other arithmetic  31 us (2%)
  starting transfers between devices  23.7 us (1%)
    reduce_scatter x4, waiting for transfers between devices, per_device(): lax.psum_scatter(lax.dot_general(up_sel, du, (((1,), (1,)), ((), ())), pr...  1440 us
    all_gather x4, waiting for transfers between devices, per_device(): full_grad = lax.all_gather(incoming, 'tp', axis=1, tiled=True)  377 us
  transfers between devices with their start and end apart: 17, of which 12 were waited for; matrix products, arithmetic and copies ran while one was open for 3% of the time, Pallas kernels for 0%

profile of v1, /device:TPU:8, one launch (start us, length us, event | category | flops | bytes accessed | tf_op | source)
XLA Modules:
  0.0 2011.4 jit_solution(10148536267386048402)
XLA Ops:
  7.2 1.3 slice_select_fusion
  10.4 26.2 %broadcast_in_dim.38 = bf16[2,4096,2,128]{3,2,1,0:T(2,128)(2,1)} broadcast(bf16[2,4096,2]{2,1,0:T(8,128)(2,1)S(1)} %bitcast.238), dimensions={0,1,2} | broadcast | bytes 4227072 | tf_op jit(solution)/shard_map/broadcast_in_dim | solution.py:20
  36.6 7.6 convert_element_type.200
  44.3 3.9 broadcast_in_dim.40
  48.2 7.3 convert_element_type.204
  55.5 6.2 bitcast_multiply_fusion.1
  61.7 1.3 copy-done.8
  62.9 2.4 bitcast_multiply_fusion
  65.4 62.4 %all-gather.12.cloned.1.call-done = bf16[1,128,4096]{1,2,0:T(8,128)(2,1)} async-done(((bf16[1,128,64]{1,2,0:T(8,128)(2,1)}), bf16[1,128,4096]{1,2,0:T(8,128)(2,1)}) %all-gather.12.cloned.1.call-update) | async-done | bytes 1048592 | tf_op jit(solution)/shard_map/all_gather | solution.py:40
  127.8 2.8 fusion.67
  130.6 3.6 fusion.24
  134.3 362.7 %reduce-scatter.5.cloned.1.call-done = f32[64,128]{1,0:T(8,128)} async-done(((f32[4096,128]{1,0:T(8,128)}), f32[64,128]{1,0:T(8,128)}) %reduce-scatter.5.cloned.1.call-update) | async-done | bytes 32784 | tf_op jit(solution)/shard_map/reduce_scatter | solution.py:51
  497.0 0.8 fusion.119
  497.7 1.9 collective-permute-start.1
  499.7 2.4 collective-permute-start
  502.1 2.6 collective-permute-done
  505.4 105.7 %all-gather.6.cloned.1.call-done = bf16[128,4096]{0,1:T(8,128)(2,1)} async-done(((bf16[128,64]{0,1:T(8,128)(2,1)}), bf16[128,4096]{0,1:T(8,128)(2,1)}) %all-gather.6.cloned.1.call-update) | async-done | bytes 1048592 | tf_op jit(solution)/shard_map/all_gather | solution.py:40
  611.1 2.8 fusion.64
  613.9 3.6 fusion.20
  617.6 362.6 %reduce-scatter.7.cloned.1.call-done = f32[64,128]{1,0:T(8,128)} async-done(((f32[4096,128]{1,0:T(8,128)}), f32[64,128]{1,0:T(8,128)}) %reduce-scatter.7.cloned.1.call-update) | async-done | bytes 32784 | tf_op jit(solution)/shard_map/reduce_scatter | solution.py:51
  980.2 0.8 fusion.122
  980.9 1.9 collective-permute-start.3
  982.8 2.4 collective-permute-start.2
  985.3 2.6 collective-permute-done.2
  988.6 105.7 %all-gather.8.cloned.1.call-done = bf16[128,4096]{0,1:T(8,128)(2,1)} async-done(((bf16[128,64]{0,1:T(8,128)(2,1)}), bf16[128,4096]{0,1:T(8,128)(2,1)}) %all-gather.8.cloned.1.call-update) | async-done | bytes 1048592 | tf_op jit(solution)/shard_map/all_gather | solution.py:40
  1094.3 2.8 fusion.61
  1097.1 3.6 fusion.16
  1101.4 1.8 stack.42
  1103.3 8.8 all-to-all-start
  1112.2 356.1 %reduce-scatter.9.cloned.1.call-done = f32[64,128]{1,0:T(8,128)} async-done(((f32[4096,128]{1,0:T(8,128)}), f32[64,128]{1,0:T(8,128)}) %reduce-scatter.9.cloned.1.call-update) | async-done | bytes 32784 | tf_op jit(solution)/shard_map/reduce_scatter | solution.py:51
  1468.2 0.8 fusion.121
  1469.0 1.9 collective-permute-start.5
  1470.9 2.4 collective-permute-start.4
  1473.3 4.5 collective-permute-done.4
  1479.8 1.1 fusion.136
  1481.0 102.7 %all-gather.10.cloned.1.call-done = bf16[128,4096]{0,1:T(8,128)(2,1)} async-done(((bf16[128,64]{0,1:T(8,128)(2,1)}), bf16[128,4096]{0,1:T(8,128)(2,1)}) %all-gather.10.cloned.1.call-update) | async-done | bytes 1048592 | tf_op jit(solution)/shard_map/all_gather | solution.py:40
  1583.7 1.1 broadcast_in_dim.49
  1585.8 2.8 fusion.3
  1588.7 1.3 copy-done.2
  1590.6 1.4 copy.26
  1592.1 1.1 broadcast_in_dim.47
  1594.3 2.8 fusion.2
  1597.1 1.3 copy-done.3
  1599.8 2.8 fusion.58
  1603.0 0.7 copy-done.9
  1605.8 0.8 fusion.4
  1606.7 1.9 copy-done.10
  1608.6 2.4 pad_maximum_fusion
  1611.0 1.3 copy-done
  1612.3 2.0 fusion.12
  1614.3 4.2 collective-permute-done.6
  1618.5 1.4 collective-permute-start.7
  1619.9 357.9 %reduce-scatter.11.cloned.1.call-done = f32[64,128]{1,0:T(8,128)} async-done(((f32[4096,128]{1,0:T(8,128)}), f32[64,128]{1,0:T(8,128)}) %reduce-scatter.11.cloned.1.call-update) | async-done | bytes 32784 | tf_op jit(solution)/shard_map/reduce_scatter | solution.py:51
  1977.8 0.8 select_bitcast_fusion.1
  1979.2 3.4 fusion.135
  1982.6 1.9 copy.27
  1984.5 1.7 reshape_squeeze.6
  1986.2 1.5 fusion.70
  1987.7 2.9 copy.28
  1990.6 1.7 reshape_squeeze.7
  1992.4 2.5 fusion.71
  1994.9 3.4 convert_element_type.248
  1999.3 2.5 copy.30
  2001.8 2.7 maximum_bitcast_fusion.1
  (116 shorter events, 14.2 us)
Async XLA Ops:
  7.2 120.6 %all-gather.12.cloned.1.call-start = ((), (), s32[]{:S(2)}) async-start(), calls=%async_computation.12 | async-start | bytes 1064960 | tf_op jit(solution)/shard_map/all_gather | solution.py:40
  8.6 488.4 %reduce-scatter.5.cloned.1.call-start = ((), (), s32[]{:S(2)}) async-start(), calls=%async_computation.5 | async-start | bytes 2129920 | tf_op jit(solution)/shard_map/reduce_scatter | solution.py:51
  55.5 6.2 copy-start.1
  55.5 7.4 copy-start.8
  62.9 64.9 %copy-start.22 = (bf16[2,1,128,256]{3,2,1,0:T(8,128)(2,1)S(1)}, bf16[2,1,128,256]{3,2,1,0:T(8,128)(2,1)}, u32[]{:S(2)}) copy-start(bf16[2,1,128,256]{3,2,1,0:T(8,128)(2,1)} %param.9) | copy-start | bytes 393220
  134.2 362.8 %copy-start.24 = (bf16[2,128,64]{1,2,0:T(8,128)(2,1)S(1)}, bf16[2,128,64]{1,2,0:T(8,128)(2,1)}, u32[]{:S(2)}) copy-start(bf16[2,128,64]{1,2,0:T(8,128)(2,1)} %param.7) | copy-start | bytes 98308
  134.2 476.9 %all-gather.6.cloned.1.call-start = ((), (), s32[]{:S(2)}) async-start(), calls=%async_computation.6 | async-start | bytes 1064960 | tf_op jit(solution)/shard_map/all_gather | solution.py:40
  497.7 4.3 collective-permute-start.1
  499.7 5.1 collective-permute-start
  505.4 474.8 %reduce-scatter.7.cloned.1.call-start = ((), (), s32[]{:S(2)}) async-start(), calls=%async_computation.7 | async-start | bytes 2129920 | tf_op jit(solution)/shard_map/reduce_scatter | solution.py:51
  617.5 362.6 %copy-start.20 = (bf16[128,64]{0,1:T(8,128)(2,1)S(1)}, bf16[128,64]{0,1:T(8,128)(2,1)}, u32[]{:S(2)}) copy-start(bf16[128,64]{0,1:T(8,128)(2,1)} %broadcast_select_fusion) | copy-start | bytes 49156
  617.5 476.8 %all-gather.8.cloned.1.call-start = ((), (), s32[]{:S(2)}) async-start(), calls=%async_computation.8 | async-start | bytes 1064960 | tf_op jit(solution)/shard_map/all_gather | solution.py:40
  980.9 7.7 copy-start.25
  980.9 4.3 collective-permute-start.3
  982.8 5.1 collective-permute-start.2
  988.5 479.7 %reduce-scatter.9.cloned.1.call-start = ((), (), s32[]{:S(2)}) async-start(), calls=%async_computation.9 | async-start | bytes 2129920 | tf_op jit(solution)/shard_map/reduce_scatter | solution.py:51
  1100.7 0.8 copy-start.29
  1103.3 364.9 %copy-start.19 = (bf16[128,64]{0,1:T(8,128)(2,1)S(1)}, bf16[128,64]{0,1:T(8,128)(2,1)}, u32[]{:S(2)}) copy-start(bf16[128,64]{0,1:T(8,128)(2,1)} %broadcast_select_fusion.1) | copy-start | bytes 49156
  1103.3 375.4 %copy-start.30 = (s32[2,1,32,2]{2,3,1,0:T(2,128)S(1)}, s32[2,1,32,2]{2,3,1,0:T(2,128)}, u32[]{:S(2)}) copy-start(s32[2,1,32,2]{2,3,1,0:T(2,128)} %param.12) | copy-start | bytes 1540
  1103.3 375.4 %copy-start.31 = (s32[2,1,2,32]{3,2,1,0:T(2,128)S(1)}, s32[2,1,2,32]{3,2,1,0:T(2,128)}, u32[]{:S(2)}) copy-start(s32[2,1,2,32]{3,2,1,0:T(2,128)} %param.13) | copy-start | bytes 1540
  1103.3 376.3 %all-to-all-start = ((bf16[64,2,128,64]{2,3,1,0:T(8,128)(2,1)}), bf16[64,2,128,64]{2,3,1,0:T(8,128)(2,1)S(1)}, u32[]{:S(2)}, u32[]{:S(2)}) async-start(bf16[64,2,128,64]{2,3,1,0:T(8,128)(2,1)} %stack.42), calls=%async_computation.4 | async-start | bytes 4194304 | tf_op jit(solution)/shard_map/all_to_all | solution.py:73
  1112.1 471.5 %all-gather.10.cloned.1.call-start = ((), (), s32[]{:S(2)}) async-start(), calls=%async_computation.10 | async-start | bytes 1064960 | tf_op jit(solution)/shard_map/all_gather | solution.py:40
  1469.0 9.8 copy-start.27
  1469.0 4.3 collective-permute-start.5
  1470.9 6.9 collective-permute-start.4
  1478.5 499.4 %reduce-scatter.11.cloned.1.call-start = ((), (), s32[]{:S(2)}) async-start(), calls=%async_computation.11 | async-start | bytes 2129920 | tf_op jit(solution)/shard_map/reduce_scatter | solution.py:51
  1479.8 103.9 %copy-start.33 = (f32[2,32]{1,0:T(2,128)S(1)}, f32[2,32]{1,0:T(2,128)}, u32[]{:S(2)}) copy-start(f32[2,32]{1,0:T(2,128)} %get-tuple-element.23) | copy-start | bytes 772
  1583.7 1.2 copy-start.11
  1583.7 1.5 copy-start.13
  1583.7 1.8 copy-start.15
  1583.7 2.1 copy-start.17
  1588.7 1.3 copy-start.2
  1590.6 1.4 copy-start.32
  1592.1 1.2 copy-start.12
  1592.1 1.5 copy-start.14
  1592.1 1.8 copy-start.16
  1592.1 2.1 copy-start.18
  1597.1 1.4 copy-start.3
  1598.6 1.2 copy-start.23
  1602.5 1.2 copy-start.9
  1604.5 1.3 copy-start.4
  1606.6 4.4 copy-start.6
  1606.6 2.0 copy-start.10
  1608.6 3.7 copy-start
  1611.0 7.5 collective-permute-start.6
  1614.3 363.5 %copy-start.21 = (bf16[128,64]{0,1:T(8,128)(2,1)S(1)}, bf16[128,64]{0,1:T(8,128)(2,1)}, u32[]{:S(2)}) copy-start(bf16[128,64]{0,1:T(8,128)(2,1)} %broadcast_select_fusion.2) | copy-start | bytes 49156
  1614.3 363.5 %copy-start.26 = (bf16[128,64]{0,1:T(8,128)(2,1)S(1)}, bf16[128,64]{0,1:T(8,128)(2,1)}, u32[]{:S(2)}) copy-start(bf16[128,64]{0,1:T(8,128)(2,1)} %copy-done.25) | copy-start | bytes 49156
  1614.3 363.5 %copy-start.28 = (bf16[128,64]{0,1:T(8,128)(2,1)S(1)}, bf16[128,64]{0,1:T(8,128)(2,1)}, u32[]{:S(2)}) copy-start(bf16[128,64]{0,1:T(8,128)(2,1)} %copy-done.27) | copy-start | bytes 49156
  1618.5 360.7 %collective-permute-start.7 = (bf16[4,2048,256]{1,2,0:T(8,128)(2,1)}, bf16[4,2048,256]{1,2,0:T(8,128)(2,1)}, u32[]{:S(2)}, u32[]{:S(2)}) collective-permute-start(bf16[4,2048,256]{1,2,0:T(8,128)(2,1)} %collective-permute-done.6), channel_id=1, source_target_pairs={{0,128},{64,192},{128,0},{192,64},{1,129},{65,193},{129,1},{193,65... | collective-permute-start | bytes 12582920 | tf_op jit(solution)/shard_map/ppermute | solution.py:16
  1994.9 3.4 copy-start.5
  1994.9 3.5 copy-start.7
Sparse Core Ops, SparseCore 0:
  12.1 115.7 all-gather.11
  134.3 362.5 reduce-scatter.4
  505.5 105.6 all-gather.5
  617.7 362.4 reduce-scatter.6
  988.7 105.5 all-gather.7
  1100.8 367.3 reduce-scatter.8
  1478.6 105.0 all-gather.9
  1614.5 363.3 reduce-scatter.10
